TPU v7x, 256 devices: a whole 4x4x8 slice. The times are simulated.
256 devices in a mesh: kv: 8 (over x, y_lo), ctx: 32 (over y_hi, z, core).
Axes of the slice: x: 4, y: 4 (y_hi: 2, y_lo: 2; y = y_hi * 2 + y_lo), z: 8, core: 2. Of those that a mesh axis runs over, the one named last changes fastest.
Arguments:
- hidden: bfloat16 [16384, 4096], P('ctx', 'kv'), may hold values from -16 to 16
- w_query: bfloat16 [4096, 4096], P(None, 'kv'), may hold values from -0.09375 to 0.09375
- w_key: bfloat16 [4096, 1024], P(None, 'kv'), may hold values from -0.09375 to 0.09375
- w_value: bfloat16 [4096, 1024], P(None, 'kv'), may hold values from -0.09375 to 0.09375
- keep_rows: int32 [2048], P('ctx'), may hold values from 0 to 511, as said below
- keep_count: int32 [32], replicated, may hold values from 32 to 64, as said below
Outputs:
- context: bfloat16 [16384, 4096], P('ctx', 'kv')
Inputs may be any that keep to these rules, and one draw needn't show every extreme that they name: `keep_rows`: the 64 slots of each block name distinct rows of that block in rising order; row 0 and row 511 of every block are always named. `keep_count`: some block has a count of 64 and some block a count of exactly 32.
All inputs are finite; a program needn't handle non-finite values.
Results may differ from a plain program's by a relative error of at most 0.015.
The roundings to bfloat16 on the way count: a program that leaves them out, or rounds other values in their place, can miss the bound.
Values may be sent and summed in bfloat16 or wider, within the bound.
A program may use at most 64 MiB of HBM per device.

v0:
```python
import math

import jax
import jax.numpy as jnp
from jax import lax
from jax.sharding import PartitionSpec as P

HD = 128


def broadcast(value, axis, source):
    kept = jnp.where(lax.axis_index(axis) == source, value, 0).astype(value.dtype)
    return lax.psum(kept, axis)


def rotate(field, places):
    half = field.shape[-1] // 2
    freq = 500000.0 ** (-(jnp.arange(half, dtype=jnp.float32) * 2.0 / field.shape[-1]))
    angles = places.astype(jnp.float32)[:, None] * freq[None, :]
    cosine = jnp.cos(angles)[:, None, :]
    sine = jnp.sin(angles)[:, None, :]
    first = field[..., :half]
    second = field[..., half:]
    return jnp.concatenate(
        [first * cosine - second * sine, second * cosine + first * sine], axis=-1
    )


def per_device(hidden, w_query, w_key, w_value, keep_rows, keep_count):
    rows = hidden.shape[0]
    groups = w_query.shape[1] // HD
    index = lax.axis_index("ctx")
    hosts = lax.axis_size("ctx")
    whole = lax.all_gather(hidden, "kv", axis=1, tiled=True)
    query_raw = jnp.dot(whole, w_query, preferred_element_type=jnp.float32)
    key_raw = jnp.dot(whole, w_key, preferred_element_type=jnp.float32)
    value_raw = jnp.dot(whole, w_value, preferred_element_type=jnp.float32)
    places = index * rows + jnp.arange(rows, dtype=jnp.int32)
    query = rotate(query_raw.reshape(rows, groups, HD), places).astype(jnp.bfloat16)
    key = rotate(key_raw.reshape(rows, 1, HD), places).reshape(rows, HD).astype(jnp.bfloat16)
    value = value_raw.astype(jnp.bfloat16)
    anchor_key, anchor_value = (broadcast(key, "ctx", 0), broadcast(value, "ctx", 0))
    kept_key = key[keep_rows]
    kept_value = value[keep_rows]
    passed_key, passed_value = (
        lax.all_gather(kept_key, "ctx", axis=0, tiled=True),
        lax.all_gather(kept_value, "ctx", axis=0, tiled=True),
    )
    keep = keep_rows.shape[0]
    slots = hosts * keep
    slot_host = jnp.arange(slots, dtype=jnp.int32) // keep
    slot_pos = jnp.arange(slots, dtype=jnp.int32) % keep
    live = (slot_pos < jnp.repeat(keep_count, keep)) & (slot_host >= 1) & (slot_host < index)
    keys = jnp.concatenate([anchor_key, passed_key, key], axis=0)
    values = jnp.concatenate([anchor_value, passed_value, value], axis=0)
    local = jnp.arange(rows, dtype=jnp.int32)
    causal = local[None, :] <= local[:, None]
    mask = jnp.concatenate(
        [
            jnp.broadcast_to(index > 0, (rows, rows)),
            jnp.broadcast_to(live[None, :], (rows, slots)),
            causal,
        ],
        axis=1,
    )

    def one_head(lane):
        scores = jnp.einsum(
            "td,sd->ts", lane, keys, preferred_element_type=jnp.float32
        ) / math.sqrt(HD)
        scores = jnp.where(mask, scores, -jnp.inf)
        top = jnp.max(scores, axis=-1, keepdims=True)
        expo = jnp.exp(scores - top)
        weights = (expo / jnp.sum(expo, axis=-1, keepdims=True)).astype(jnp.bfloat16)
        return jnp.dot(weights, values, preferred_element_type=jnp.float32)

    heads_out = lax.map(one_head, jnp.moveaxis(query, 1, 0))
    return jnp.moveaxis(heads_out, 0, 1).reshape(rows, groups * HD).astype(jnp.bfloat16)


def solution(mesh):
    in_specs = (P("ctx", "kv"), P(None, "kv"), P(None, "kv"), P(None, "kv"), P("ctx"), P())
    out_specs = P("ctx", "kv")
    return jax.shard_map(
        per_device, mesh=mesh, in_specs=in_specs, out_specs=out_specs, check_vma=False
    )
```

profile of v0, /device:TPU:1, one launch (start us, length us, event | category | flops | bytes accessed | tf_op | source)
XLA Modules:
  0.0 468.6 jit_solution(4093867214732488162)
XLA Ops:
  6.5 0.7 all-gather.4.cloned.1.call-update
  7.3 0.0 all-reduce.3.cloned.1.call-start
  7.3 0.7 broadcast_in_dim.48
  8.1 0.1 reshape.152
  8.2 0.7 compare_select_fusion
  8.9 0.1 iota_compare_fusion
  8.9 1.8 multiply_cosine_fusion
  10.7 0.5 pad_add_fusion
  11.2 94.1 %all-gather.4.cloned.1.call-done = bf16[512,4096]{1,0:T(8,128)(2,1)} async-done(((bf16[512,512]{1,0:T(8,128)(2,1)}), bf16[512,4096]{1,0:T(8,128)(2,1)}) %all-gather.4.cloned.1.call-update) | async-done | bytes 4194320 | tf_op jit(solution)/shard_map/all_gather | solution.py:34
  105.2 4.0 convolution_bitcast_fusion
  109.2 0.6 fusion.12
  109.8 0.7 broadcast_select_fusion.1
  110.5 0.1 copy.9
  110.6 0.6 gather_fusion
  111.3 46.6 %all-gather = bf16[2048,128]{1,0:T(8,128)(2,1)} all-gather(bf16[64,128]{1,0:T(8,128)(2,1)S(1)} %gather_fusion), channel_id=2, replica_groups=mesh['kv'=8,'ctx'=32] {'ctx'}, dimensions={0}, use_global_device_ids=true | all-gather | bytes 540672 | tf_op jit(solution)/shard_map/all_gather | solution.py:46
  157.8 5.8 %fusion.27 = f32[512,512]{0,1:T(8,128)S(1)} fusion(bf16[512,4096]{1,0:T(8,128)(2,1)} %all-gather.4.cloned.1.call-done, bf16[4096,512]{1,0:T(8,128)(2,1)} %param.9), kind=kOutput, calls=%fused_computation.60 | convolution fusion | flops 2147483648 | bytes 9437184 | tf_op jit(solution)/shard_map/dot_general | solution.py:35
  163.7 0.9 fusion.26
  164.6 2.4 copy.18
  166.9 1.3 copy.19
  168.2 4.4 broadcast_select_fusion
  172.7 1.8 subtract_convert_fusion
  174.5 1.1 maximum_bitcast_fusion
  175.6 0.1 copy.13
  175.7 0.6 gather_fusion.1
  176.3 41.0 %all-gather.1 = bf16[2048,128]{1,0:T(8,128)(2,1)} all-gather(bf16[64,128]{1,0:T(8,128)(2,1)S(1)} %gather_fusion.1), channel_id=3, replica_groups=mesh['kv'=8,'ctx'=32] {'ctx'}, dimensions={0}, use_global_device_ids=true | all-gather | bytes 540672 | tf_op jit(solution)/shard_map/all_gather | solution.py:47
  217.3 215.0 %all-reduce.3.cloned.1.call-done = (bf16[512,128]{0,1:T(8,128)(2,1)}, bf16[512,128]{0,1:T(8,128)(2,1)}) async-done(((bf16[512,128]{0,1:T(8,128)(2,1)}, bf16[512,128]{0,1:T(8,128)(2,1)}), (bf16[512,128]{0,1:T(8,128)(2,1)}, bf16[512,128]{0,1:T(8,128)(2,1)})) %all-reduce.3.cloned.1.call-update) | async-done | bytes 262160 | tf_op jit(solution)/shard_map/psum | solution.py:13
  432.3 1.7 copy.10
  434.0 1.6 copy.14
  435.6 1.1 pad_maximum_fusion
  436.7 2.1 pad_maximum_fusion.1
  438.8 21.1 %while.10 = (s32[]{:T(128)}, bf16[4,512,128]{2,1,0:T(8,128)(2,1)}, bf16[4,512,128]{2,1,0:T(8,128)(2,1)}, bf16[3072,128]{1,0:T(8,128)(2,1)S(1)}, pred[512,3072]{1...) while((s32[]{:T(128)}, bf16[4,512,128]{2,1,0:T(8,128)(2,1)}, bf16[4,512,128]{2,1,0:T(8,128)(2,1)}, ...), condition=%wide.region_5.6_spmd, body=%wide.region_2.5_spmd.sunk | while | flops 817888256 | bytes 25570408 | solution.py:77
  438.8 2.3 fusion.44
  441.1 1.0 fusion.45
  442.1 0.1 copy-done.3
  442.2 1.8 fusion.46
  444.0 2.3 fusion.44
  446.3 1.0 fusion.45
  447.3 0.1 copy-done.3
  447.5 1.9 fusion.46
  449.3 2.3 fusion.44
  451.6 1.0 fusion.45
  452.6 0.1 copy-done.3
  452.7 1.9 fusion.46
  454.6 2.3 fusion.44
  456.8 1.0 fusion.45
  457.8 0.1 copy-done.3
  458.0 1.9 fusion.46
  459.8 1.9 copy_bitcast_fusion
  (20 shorter events, 0.1 us)
Async XLA Ops:
  6.5 161.7 %copy-start = (bf16[4096,128]{1,0:T(8,128)(2,1)S(1)}, bf16[4096,128]{1,0:T(8,128)(2,1)}, u32[]{:S(2)}) copy-start(bf16[4096,128]{1,0:T(8,128)(2,1)} %param.11) | copy-start | bytes 3145732
  6.5 98.7 %all-gather.4.cloned.1.call-start = ((), (), s32[]{:S(2)}) async-start(), calls=%async_computation | async-start | bytes 4718592 | tf_op jit(solution)/shard_map/all_gather | solution.py:34
  7.3 425.0 %all-reduce.3.cloned.1.call-start = ((), (), s32[]{:S(2)}) async-start(), calls=%async_computation.1 | async-start | bytes 524288 | tf_op jit(solution)/shard_map/psum | solution.py:13
  168.2 4.4 copy-start.2
  175.7 258.3 %copy-start.1 = (bf16[512,128]{1,0:T(8,128)(2,1)}, bf16[512,128]{1,0:T(8,128)(2,1)S(1)}, u32[]{:S(2)}) copy-start(bf16[512,128]{1,0:T(8,128)(2,1)S(1)} %copy.13) | copy-start | bytes 393220
  441.1 1.1 copy-start.3
  446.3 1.1 copy-start.3
  451.6 1.1 copy-start.3
  456.8 1.1 copy-start.3
Sparse Core Ops, SparseCore 0:
  9.2 96.0 all-gather.3
  172.8 259.4 all-reduce.2
where the time goes:
time: 469 us
  waiting for transfers between devices  310 us (66%)
  blocking collectives  87.5 us (19%)
  matrix products  30.7 us (7%)
  other arithmetic  14.3 us (3%)
  between operations  13.5 us (3%)
  local copies, waits for them, and re-layouts  12.7 us (3%)
    psum x1, waiting for transfers between devices, broadcast(): return lax.psum(kept, axis)  215 us
    all_gather x1, waiting for transfers between devices, per_device(): whole = lax.all_gather(hidden, 'kv', axis=1, tiled=True)  94.1 us
    all_gather x1, blocking collectives, per_device(): lax.all_gather(kept_key, 'ctx', axis=0, tiled=True)  46.6 us
    all_gather x1, blocking collectives, per_device(): lax.all_gather(kept_value, 'ctx', axis=0, tiled=True)  41 us
  transfers between devices with their start and end apart: 2, of which 2 were waited for; matrix products, arithmetic and copies ran while one was open for 2% of the time, Pallas kernels for 0%

commit v1 on v0

v1 whole, which is shorter than its diff:
```python
import functools
import math

import jax
import jax.numpy as jnp
import numpy as np
from jax import lax
from jax.experimental import pallas as pl
from jax.experimental.pallas import tpu as pltpu
from jax.sharding import PartitionSpec as P

HD = 128
MESH = pl.DeviceIdType.MESH
BF = jnp.bfloat16
F32 = jnp.float32
SCALE = math.log2(math.e) / math.sqrt(HD)
TILE = 512


class Wire:
    def __init__(self, send, recv):
        self.send, self.recv, self.copies = send, recv, []

    def go(self, src, dst, device):
        n = len(self.copies)
        copy = pltpu.make_async_remote_copy(
            src_ref=src,
            dst_ref=dst,
            send_sem=self.send.at[n],
            recv_sem=self.recv.at[n],
            device_id=device,
            device_id_type=MESH,
        )
        copy.start()
        self.copies.append(copy)
        return copy


def up16(n):
    return (n + 15) // 16 * 16


class Gather:
    def __init__(self, wire, buf, base, rows, cut, kv_at, source=None):
        self.wire, self.buf, self.base, self.rows, self.cut, self.at = wire, buf, base, rows, cut, kv_at
        me = kv_at(0, 0)
        self.source = buf.at[me, pl.ds(base, rows)] if source is None else source

    def part(self, dx, dy, lo, hi):
        return self.buf.at[self.at(dx, dy), pl.ds(self.base + lo, hi - lo)]

    def fwd(self, part, dx, dy):
        return self.wire.go(part, part, {"kv": self.at(dx, dy)})

    def own(self):
        dst = self.part(0, 0, 0, self.rows)
        self.first = [
            self.wire.go(self.source, dst, {"kv": self.at(dx, dy)}) for dx, dy in ((1, 0), (3, 0), (0, 1))
        ]

    def second(self):
        n, cut, half = self.rows, self.cut, up16(self.rows // 2)
        from_left, from_right, from_y = self.first
        from_y.wait_recv()
        part = self.part(0, 1, cut, n)
        self.b_left = self.fwd(part, 1, 0)
        self.b_right = self.fwd(part, 3, 0)
        from_left.wait_recv()
        self.far0 = self.fwd(self.part(3, 0, 0, half), 1, 0)
        self.y_left = self.fwd(self.part(3, 0, 0, cut), 0, 1)
        from_right.wait_recv()
        self.far1 = self.fwd(self.part(1, 0, half, n), 3, 0)
        self.y_right = self.fwd(self.part(1, 0, 0, cut), 0, 1)

    def third(self):
        n, cut = self.rows, self.cut
        mid = cut + up16((n - cut) // 2)
        self.b_left.wait_recv()
        self.bfar0 = self.fwd(self.part(3, 1, cut, mid), 1, 0)
        self.b_right.wait_recv()
        self.bfar1 = self.fwd(self.part(1, 1, mid, n), 3, 0)
        self.far0.wait_recv()
        self.far1.wait_recv()
        self.y_far = self.fwd(self.part(2, 0, 0, cut), 0, 1)

    def finish(self):
        for copy in (self.y_left, self.y_right, self.bfar0, self.bfar1, self.y_far):
            copy.wait_recv()


def rope(field, cosine, sine):
    return field * cosine + pltpu.roll(field, HD // 2, 1) * sine


def tables(places, freq, sign):
    angles = places * freq
    return jnp.cos(angles), jnp.sin(angles) * sign


def kernel(
    sizes,
    hidden, w_query, w_key, w_value, keep_rows, keep_count, freq,
    out,
    H, RH, W, G, KR, VR, KL, VL, Q, S, cos_t, sin_t, freq_v, out_v,
    send, recv, a_send, a_recv, l_sem,
):
    rows, keep, share, groups, n_ctx, nz = sizes
    chunk = 128
    n_chunks = rows // chunk
    slots = keep + share
    kv = lax.axis_index("kv")
    ctx = lax.axis_index("ctx")
    kx, ky = kv // 2, kv % 2
    yh, z, core = ctx // (2 * nz), (ctx // 2) % nz, ctx % 2

    def kv_at(dx, dy):
        return ((kx + dx) % 4) * 2 + (ky + dy) % 2

    def ctx_at(dy, dz, dc):
        return ((yh + dy) % 2) * (2 * nz) + ((z + dz) % nz) * 2 + (core + dc) % 2

    local = []

    def fetch(src, dst):
        copy = pltpu.make_async_copy(src, dst, l_sem.at[len(local)])
        copy.start()
        local.append(copy)
        return copy

    own_here = fetch(hidden, H.at[kv])
    got_freq = fetch(freq, freq_v)
    got_w = [
        fetch(w_key, W.at[:, pl.ds(groups * HD, HD)]),
        fetch(w_value, W.at[:, pl.ds((groups + 1) * HD, HD)]),
        fetch(w_query, W.at[:, pl.ds(0, groups * HD)]),
    ]

    barrier = pltpu.get_barrier_semaphore()
    kv_near = ((1, 0), (3, 0), (0, 1))
    ctx_near = ((1, 0, 0), (0, 1, 0), (0, nz - 1, 0), (0, 2, 0), (0, nz - 2, 0), (0, 0, 1))
    for step in kv_near:
        pl.semaphore_signal(barrier, inc=1, device_id={"kv": kv_at(*step)}, device_id_type=MESH)
    for step in ctx_near:
        pl.semaphore_signal(barrier, inc=1, device_id={"ctx": ctx_at(*step)}, device_id_type=MESH)

    @pl.when(ctx != 0)
    def _():
        pl.semaphore_signal(barrier, inc=1, device_id={"ctx": 0}, device_id_type=MESH)

    near = len(kv_near) + len(ctx_near)
    pl.semaphore_wait(barrier, jnp.where(ctx == 0, near + n_ctx - 1, near))

    wire = Wire(send, recv)
    anchor_slot = RH.at[kv, pl.ds(keep, share)]

    def anchor_copy(c):
        return pltpu.make_async_remote_copy(
            src_ref=hidden.at[pl.ds(c * share, share)],
            dst_ref=anchor_slot,
            send_sem=a_send.at[c],
            recv_sem=a_recv,
            device_id={"ctx": c},
            device_id_type=MESH,
        )

    @pl.when(ctx == 0)
    def _():
        def body(c, carry):
            anchor_copy(c).start()
            return carry

        lax.fori_loop(1, n_ctx, body, 0)
        mine = pltpu.make_async_copy(hidden.at[pl.ds(0, share)], anchor_slot, a_recv)
        mine.start()

    parts = [
        Gather(wire, H, r * chunk, chunk, 64, kv_at, hidden.at[pl.ds(r * chunk, chunk)]) for r in range(n_chunks)
    ]
    extra = Gather(wire, RH, 0, slots, 32, kv_at)
    parts[0].own()

    place_of = lax.broadcasted_iota(jnp.int32, (keep, HD), 0)
    picked = jnp.zeros((keep, HD), jnp.int32)
    for j in range(keep):
        picked = jnp.where(place_of == j, keep_rows[j], picked)
    lanes = lax.broadcasted_iota(jnp.int32, (keep, HD), 1)
    one_hot = jnp.concatenate(
        [(lanes + k * HD == picked).astype(F32).astype(BF) for k in range(rows // HD)], axis=1
    )
    own_here.wait()
    RH[kv, 0:keep] = jnp.dot(one_hot, H[kv], preferred_element_type=F32).astype(BF)
    anchor_copy(0).wait_recv()
    extra.own()
    parts[1].own()

    got_freq.wait()
    freq_row = freq_v[0:1, :]
    lane = lax.broadcasted_iota(jnp.int32, (1, HD), 1)
    sign = jnp.where(lane < HD // 2, -1.0, 1.0)

    def table_of(i, carry):
        at = pl.ds(pl.multiple_of(i * 64, 64), 64)
        places = (ctx * rows + i * 64 + lax.broadcasted_iota(jnp.int32, (64, HD), 0)).astype(F32)
        cos_t[at, :], sin_t[at, :] = tables(places, freq_row, sign)
        return carry

    parts[0].second()
    extra.second()
    lax.fori_loop(0, rows // 64, table_of, 0)
    extra_places = jnp.concatenate(
        [
            (ctx * rows + picked).astype(F32),
            (ctx * share + lax.broadcasted_iota(jnp.int32, (share, HD), 0)).astype(F32),
        ],
        axis=0,
    )
    extra_cos, extra_sin = tables(extra_places, freq_row, sign)
    parts[0].third()
    extra.third()
    parts[2].own()
    for copy in got_w:
        copy.wait()
    depth = hidden.shape[1]
    n_src = H.shape[0]
    extra.finish()
    kv_cols = slice(groups * HD, (groups + 2) * HD)
    raw = jnp.zeros((slots, 2 * HD), F32)
    for s in range(n_src):
        raw += jnp.dot(RH[s], W[s * depth : (s + 1) * depth, kv_cols], preferred_element_type=F32)
    G[core, z, yh, :, 0:HD] = rope(raw[:, :HD], extra_cos, extra_sin).astype(BF)
    G[core, z, yh, :, HD:] = raw[:, HD:].astype(BF)

    def hop(part, step):
        return wire.go(part, part, {"ctx": ctx_at(*step)})

    def at_z(dz):
        return G.at[core, (z + dz) % nz]

    across = hop(G.at[core, z, yh], (1, 0, 0))
    parts[1].second()

    def project(r):
        part = slice(r * chunk, (r + 1) * chunk)
        raw = jnp.zeros((chunk, (groups + 2) * HD), F32)
        for s in range(n_src):
            raw += jnp.dot(H[s, part], W[s * depth : (s + 1) * depth], preferred_element_type=F32)
        cosine, sine = cos_t[part], sin_t[part]
        for g in range(groups):
            Q[r, g * chunk : (g + 1) * chunk] = rope(raw[:, g * HD : (g + 1) * HD], cosine, sine).astype(BF)
        KL[part] = rope(raw[:, groups * HD : (groups + 1) * HD], cosine, sine).astype(BF)
        VL[part, 0:HD] = raw[:, (groups + 1) * HD :].astype(BF)
        VL[part, HD:] = jnp.ones((chunk, HD), BF)

    across.wait_recv()
    pair = at_z(0)
    near_z = {dz: hop(pair, (0, dz, 0)) for dz in (1, nz - 1, 2, nz - 2)}
    to_core = [hop(pair, (0, 0, 1))]
    parts[0].finish()
    project(0)
    parts[1].third()
    parts[3].own()

    far = []
    for dz, half in ((2, 0), (nz - 2, 1)):
        near_z[dz].wait_recv()
        got = at_z(nz - dz)
        one = 1 if dz == 2 else nz - 1
        far.append((hop(got, (0, one, 0)), one))
        far.append((hop(G.at[core, (z + nz - dz) % nz, half], (0, dz, 0)), half))
        to_core.append(hop(got, (0, 0, 1)))
    for dz in (1, nz - 1):
        near_z[dz].wait_recv()
        to_core.append(hop(at_z(nz - dz), (0, 0, 1)))
    parts[2].second()
    parts[1].finish()
    project(1)
    for i, dz in ((0, 3), (2, nz - 3)):
        far[i][0].wait_recv()
        to_core.append(hop(at_z(nz - dz), (0, 0, 1)))
    for i, half in ((1, 0), (3, 1)):
        far[i][0].wait_recv()
        to_core.append(hop(G.at[core, (z + nz // 2) % nz, half], (0, 0, 1)))
    parts[2].third()
    parts[3].second()
    for copy in to_core:
        copy.wait_recv()

    first_key = KL[0:16].astype(F32)[0:1]
    row_of = lax.broadcasted_iota(jnp.int32, (slots, HD), 0)

    def ready(i, carry):
        c = (i % 2) * (2 * nz) + ((i // 2) % nz) * 2 + i // (2 * nz)
        limit = jnp.where((c >= 1) & (c < ctx), keep_count[c], 0)
        limit_a = jnp.where(ctx >= 1, slots, 0)
        live = row_of < jnp.where(row_of < keep, limit, limit_a)
        block = G[i // (2 * nz), (i // 2) % nz, i % 2].astype(F32)
        at = pl.ds(pl.multiple_of(i * slots, 16), slots)
        KR[at, :] = jnp.where(live, block[:, :HD], first_key).astype(BF)
        VR[at, 0:HD] = jnp.where(live, block[:, HD:], 0.0).astype(BF)
        VR[at, HD:] = live.astype(F32).astype(BF)
        return carry

    lax.fori_loop(0, n_ctx, ready, 0)

    many = groups * chunk
    n_far = n_ctx * slots
    contract = (((1,), (1,)), ((), ()))
    in_chunk = lax.broadcasted_iota(jnp.int32, (many, chunk), 0) % chunk
    causal = lax.broadcasted_iota(jnp.int32, (many, chunk), 1) <= in_chunk

    def lane_max(s):
        top = s[:, :HD]
        for k in range(1, s.shape[1] // HD):
            top = jnp.maximum(top, s[:, k * HD : (k + 1) * HD])
        return top

    def attend(r):
        q = Q[r]
        near_keys = (r + 1) * chunk

        def scores(keys):
            return lax.dot_general(q, keys, contract, preferred_element_type=F32) * SCALE

        s = scores(KL[0:near_keys])
        diagonal = jnp.where(causal, s[:, r * chunk :], -jnp.inf)
        top = diagonal
        if r:
            s = s[:, : r * chunk]
            S[:, n_far : n_far + r * chunk] = s
            top = jnp.maximum(top, lane_max(s))
        S[:, n_far + r * chunk : n_far + near_keys] = diagonal

        def first(i, top):
            at = pl.ds(pl.multiple_of(i * TILE, TILE), TILE)
            s = scores(KR[at, :])
            S[:, at] = s
            return jnp.maximum(top, lane_max(s))

        top = lax.fori_loop(0, n_far // TILE, first, top)
        top = jnp.max(top, axis=1, keepdims=True)

        def weigh(s, values):
            return jnp.dot(jnp.exp2(s - top).astype(BF), values, preferred_element_type=F32)

        total = weigh(S[:, n_far : n_far + near_keys], VL[0:near_keys])

        def second(i, total):
            at = pl.ds(pl.multiple_of(i * TILE, TILE), TILE)
            return total + weigh(S[:, at], VR[at, :])

        total = lax.fori_loop(0, n_far // TILE, second, total)
        result = (total[:, :HD] / total[:, HD:]).astype(BF)
        part = slice(r * chunk, (r + 1) * chunk)
        for g in range(groups):
            out_v[part, g * HD : (g + 1) * HD] = result[g * chunk : (g + 1) * chunk]
        return fetch(out_v.at[part], out.at[part])

    parts[2].finish()
    project(2)
    written = [attend(0)]
    parts[3].third()
    written += [attend(1), attend(2)]
    parts[3].finish()
    project(3)
    written.append(attend(3))
    for copy in written:
        copy.wait()
    for copy in wire.copies:
        copy.wait_send()

    @pl.when(ctx == 0)
    def _():
        def body(c, carry):
            anchor_copy(c).wait_send()
            return carry

        lax.fori_loop(1, n_ctx, body, 0)


def per_device(n_kv, n_ctx, hidden, w_query, w_key, w_value, keep_rows, keep_count):
    rows, depth = hidden.shape
    keep = keep_rows.shape[0]
    groups = w_query.shape[1] // HD
    nz = n_ctx // 4
    share = rows // n_ctx
    slots = keep + share
    freq = 500000.0 ** (-(np.arange(HD // 2, dtype=np.float64) * 2.0 / HD))
    freq = jnp.asarray(np.broadcast_to(np.concatenate([freq, freq]), (8, HD)), F32)
    any_spec = pl.BlockSpec(memory_space=pl.ANY)
    smem = pl.BlockSpec(memory_space=pltpu.SMEM)
    n_far = n_ctx * slots
    return pl.pallas_call(
        functools.partial(kernel, (rows, keep, share, groups, n_ctx, nz)),
        out_shape=jax.ShapeDtypeStruct((rows, groups * HD), BF),
        in_specs=[any_spec] * 4 + [smem, smem, any_spec],
        out_specs=any_spec,
        scratch_shapes=[
            pltpu.VMEM((n_kv, rows, depth), BF),
            pltpu.VMEM((n_kv, slots, depth), BF),
            pltpu.VMEM((n_kv * depth, (groups + 2) * HD), BF),
            pltpu.VMEM((2, nz, 2, slots, 2 * HD), BF),
            pltpu.VMEM((n_far, HD), BF),
            pltpu.VMEM((n_far, 2 * HD), BF),
            pltpu.VMEM((rows, HD), BF),
            pltpu.VMEM((rows, 2 * HD), BF),
            pltpu.VMEM((rows // 128, groups * 128, HD), BF),
            pltpu.VMEM((groups * 128, n_far + rows), F32),
            pltpu.VMEM((rows, HD), F32),
            pltpu.VMEM((rows, HD), F32),
            pltpu.VMEM((8, HD), F32),
            pltpu.VMEM((rows, groups * HD), BF),
            pltpu.SemaphoreType.DMA((96,)),
            pltpu.SemaphoreType.DMA((96,)),
            pltpu.SemaphoreType.DMA((n_ctx,)),
            pltpu.SemaphoreType.DMA,
            pltpu.SemaphoreType.DMA((16,)),
        ],
        compiler_params=pltpu.CompilerParams(
            collective_id=0, has_side_effects=True, vmem_limit_bytes=58 << 20
        ),
        name="prefill",
    )(hidden, w_query, w_key, w_value, keep_rows, keep_count, freq)


def solution(mesh):
    in_specs = (P("ctx", "kv"), P(None, "kv"), P(None, "kv"), P(None, "kv"), P("ctx"), P())
    out_specs = P("ctx", "kv")
    step = functools.partial(per_device, mesh.shape["kv"], mesh.shape["ctx"])
    return jax.shard_map(step, mesh=mesh, in_specs=in_specs, out_specs=out_specs, check_vma=False)
```

time: 469 us -> 80.5 us (0.17)
  waiting for transfers between devices: 310 us -> 0 us
  blocking collectives: 87.5 us -> 0 us
  Pallas kernels: 0 us -> 78.5 us
  matrix products: 30.7 us -> 0 us
  other arithmetic: 14.3 us -> 0 us
  between operations: 13.5 us -> 0.01 us
  local copies, waits for them, and re-layouts: 12.7 us -> 1.87 us
    psum x1 -> x0, waiting for transfers between devices: 215 us -> none  [broadcast(): return lax.psum(kept, axis)]
    all_gather x1 -> x0, waiting for transfers between devices: 94.1 us -> none  [per_device(): whole = lax.all_gather(hidden, 'kv', axis=1, tiled=True)]
    all_gather x2 -> x0, blocking collectives: 87.5 us -> none  [the longest x1 46.6 us: per_device(): lax.all_gather(kept_key, 'ctx', axis=0, tiled=True)]
    pallas_call x0 -> x1, Pallas kernels: none -> 78.5 us  [per_device(): pl.pallas_call(functools.partial(kernel, (rows, keep, share, groups, n_ct...]
    dot_general x11 -> x0, matrix products: 30.7 us -> none  [the longest x4 9.07 us: one_head(): jnp.einsum('td,sd->ts', lane, keys, preferred_element_type=jnp.float32)]
  transfers between devices with their start and end apart: 2 -> 0, of which waited for: 2 -> 0; matrix products, arithmetic and copies ran while one was open for 2% -> 0% of each run, Pallas kernels for 0% -> 0%
where the time goes in v1:
time: 80.5 us; the launch traced here: 80.4 us
  Pallas kernels  78.5 us (98%)
  local copies, waits for them, and re-layouts  1.87 us (2%)
    pallas_call x1, Pallas kernels, per_device(): pl.pallas_call(functools.partial(kernel, (rows, keep, share, groups, n_ct...  78.5 us
    unnamed x1, local copies, waits for them, and re-layouts  1.87 us

profile of v1, /device:TPU:1, one launch (start us, length us, event | category | flops | bytes accessed | tf_op | source)
XLA Modules:
  0.0 80.4 jit_solution(7629348463371310233)
XLA Ops:
  0.0 78.5 %prefill.1 = bf16[512,512]{1,0:T(8,128)(2,1)} custom-call(bf16[512,512]{1,0:T(8,128)(2,1)} %hidden.1, bf16[4096,512]{1,0:T(8,128)(2,1)} %w_query.1, bf16[4096,128]{1,0:T(8,128)(2,1)} %w_key.1, bf16[4096,128]{1,0:T(8,128)(2,1)} %w_value.1, s32[64]{0:T(128)} %keep_rows.1, s32[32]{0:T(128)} %keep_count.1, f32[8,128]{1,0:T(8,128)} %constant.2.clone.freq), custom_call_target="tpu_custom_call" | custom-call | tf_op jit(solution)/shard_map/prefill/pallas_call | solution.py:392
  78.5 1.9 %copy.9 = bf16[512,512]{1,0:T(8,128)(2,1)} copy(bf16[512,512]{1,0:T(8,128)(2,1)} %prefill.1) | data formatting | bytes 1048576

commit v2 on v0

v2 whole, which is shorter than its diff:
```python
import functools
import math

import jax
import jax.numpy as jnp
import numpy as np
from jax import lax
from jax.experimental import pallas as pl
from jax.experimental.pallas import tpu as pltpu
from jax.sharding import PartitionSpec as P

HD = 128
MESH = pl.DeviceIdType.MESH
BF = jnp.bfloat16
F32 = jnp.float32
SCALE = math.log2(math.e) / math.sqrt(HD)


def up16(n):
    return (n + 15) // 16 * 16


def send(part, dst, device, send_sem, recv_sem):
    copy = pltpu.make_async_remote_copy(
        src_ref=part, dst_ref=dst, send_sem=send_sem, recv_sem=recv_sem, device_id=device, device_id_type=MESH
    )
    copy.start()
    return copy


def take(like, sem):
    pltpu.make_async_copy(like, like, sem).wait()


class Gather:
    def __init__(self, sems, index, like, buf, base, rows, cut, kv_at, source):
        self.buf, self.base, self.rows, self.cut, self.at, self.source = buf, base, rows, cut, kv_at, source
        self.send_sem, self.recv = sems[0].at[index], [sems[1].at[index, i] for i in range(7)]
        self.like = like

    def part(self, dx, dy, lo, hi):
        return self.buf.at[self.at(dx, dy), pl.ds(self.base + lo, hi - lo)]

    def fwd(self, part, dx, dy, sem):
        return send(part, part, {"kv": self.at(dx, dy)}, self.send_sem, self.recv[sem])

    def own(self, ways=(0, 1, 2)):
        dst = self.part(0, 0, 0, self.rows)
        for i in ways:
            device = {"kv": self.at(*((1, 0), (3, 0), (0, 1))[i])}
            send(self.source, dst, device, self.send_sem, self.recv[i])

    def took(self, rows, sem):
        take(self.like.at[0, pl.ds(0, rows)], self.recv[sem])

    def second(self):
        n, cut, half = self.rows, self.cut, up16(self.rows // 2)
        self.took(n, 2)
        part = self.part(0, 1, cut, n)
        self.fwd(part, 1, 0, 3)
        self.fwd(part, 3, 0, 4)
        self.took(n, 0)
        self.fwd(self.part(3, 0, 0, half), 1, 0, 5)
        self.fwd(self.part(3, 0, 0, cut), 0, 1, 6)
        self.took(n, 1)
        self.fwd(self.part(1, 0, half, n), 3, 0, 5)
        self.fwd(self.part(1, 0, 0, cut), 0, 1, 6)

    def third(self):
        n, cut = self.rows, self.cut
        mid = cut + up16((n - cut) // 2)
        self.took(n - cut, 3)
        self.fwd(self.part(3, 1, cut, mid), 1, 0, 6)
        self.took(n - cut, 4)
        self.fwd(self.part(1, 1, mid, n), 3, 0, 6)
        self.took(n, 5)
        self.fwd(self.part(2, 0, 0, cut), 0, 1, 6)

    def finish(self):
        self.took(self.rows + 2 * self.cut, 6)

    def sent(self):
        take(self.like.at[0:7, pl.ds(0, self.rows)], self.send_sem)


def rope(field, cosine, sine):
    return field * cosine + pltpu.roll(field, HD // 2, 1) * sine


def tables(places, freq, sign):
    angles = places * freq
    return jnp.cos(angles), jnp.sin(angles) * sign


def lane_fold(op, s, total):
    for k in range(0, s.shape[1], HD):
        total = op(total, s[:, k : k + HD])
    return total


def kernel(
    sizes,
    hidden, w_query, w_key, w_value, keep_rows, keep_count, freq,
    out,
    H, RH, W, G, bias, KL, VL, Q, S, cos_t, sin_t, freq_v, out_v,
    k_send, k_recv, a_sem, c_send, c_recv, l_sem,
):
    rows, keep, share, groups, n_ctx, nz = sizes
    chunk = 128
    n_chunks = rows // chunk
    slots = keep + share
    depth = hidden.shape[1]
    n_src = H.shape[0]
    many = groups * chunk
    n_far = n_ctx * slots
    kv = lax.axis_index("kv")
    ctx = lax.axis_index("ctx")
    kx, ky = kv // 2, kv % 2
    yh, z, core = ctx // (2 * nz), (ctx // 2) % nz, ctx % 2

    def kv_at(dx, dy):
        return ((kx + dx) % 4) * 2 + (ky + dy) % 2

    def ctx_at(dy, dz, dc):
        return ((yh + dy) % 2) * (2 * nz) + ((z + dz) % nz) * 2 + (core + dc) % 2

    def fetch(src, dst, sem):
        copy = pltpu.make_async_copy(src, dst, l_sem.at[sem])
        copy.start()
        return copy

    barrier = pltpu.get_barrier_semaphore()
    kv_near = [(dx, dy) for dx in range(4) for dy in range(2) if dx or dy]
    ctx_near = ((1, 0, 0), (0, 1, 0), (0, nz - 1, 0), (0, 2, 0), (0, nz - 2, 0), (0, 0, 1))

    @pl.when(ctx != 0)
    def _():
        pl.semaphore_signal(barrier, inc=1, device_id={"ctx": 0}, device_id_type=MESH)

    for step in ctx_near:
        pl.semaphore_signal(barrier, inc=1, device_id={"ctx": ctx_at(*step)}, device_id_type=MESH)
    for step in kv_near:
        pl.semaphore_signal(barrier, inc=1, device_id={"kv": kv_at(*step)}, device_id_type=MESH)

    own_here = fetch(hidden, H.at[kv], 0)
    got_freq = fetch(freq, freq_v, 1)
    fetch(w_key, W.at[:, pl.ds(groups * HD, HD)], 2)
    fetch(w_value, W.at[:, pl.ds((groups + 1) * HD, HD)], 2)
    fetch(w_query, W.at[:, pl.ds(0, groups * HD)], 2)

    place_of = lax.broadcasted_iota(jnp.int32, (keep, HD), 0)
    picked = jnp.zeros((keep, HD), jnp.int32)
    for j in range(keep):
        picked = jnp.where(place_of == j, keep_rows[j], picked)
    lanes = lax.broadcasted_iota(jnp.int32, (keep, HD), 1)
    one_hot = jnp.concatenate(
        [(lanes + k * HD == picked).astype(F32).astype(BF) for k in range(rows // HD)], axis=1
    )
    own_here.wait()
    RH[kv, 0:keep] = jnp.dot(one_hot, H[kv], preferred_element_type=F32).astype(BF)

    near = len(kv_near) + len(ctx_near)
    pl.semaphore_wait(barrier, jnp.where(ctx == 0, near + n_ctx - 1, near))

    anchor_slot = RH.at[kv, pl.ds(keep, share)]

    def anchor_copy(c):
        return pltpu.make_async_remote_copy(
            src_ref=hidden.at[pl.ds(c * share, share)],
            dst_ref=anchor_slot,
            send_sem=a_sem.at[0],
            recv_sem=a_sem.at[1],
            device_id={"ctx": c},
            device_id_type=MESH,
        )

    @pl.when(ctx == 0)
    def _():
        def body(c, carry):
            anchor_copy(c).start()
            return carry

        lax.fori_loop(1, n_ctx, body, 0)
        mine = pltpu.make_async_copy(hidden.at[pl.ds(0, share)], anchor_slot, a_sem.at[1])
        mine.start()

    sems = (k_send, k_recv)
    extra = Gather(sems, n_chunks, H, RH, 0, keep, keep // 2, kv_at, RH.at[kv, pl.ds(0, keep)])
    parts = [
        Gather(sems, r, H, H, r * chunk, chunk, (48, 64)[r >= n_chunks // 2], kv_at, hidden.at[pl.ds(r * chunk, chunk)])
        for r in range(n_chunks)
    ]
    extra.own()

    KL[...] = jnp.zeros_like(KL)
    VL[...] = jnp.zeros_like(VL)
    row_of = lax.broadcasted_iota(jnp.int32, (slots, HD), 0)
    first_lane = lax.broadcasted_iota(jnp.int32, (slots, HD), 1) == 0

    def mark(i, carry):
        c = (i % 2) * (2 * nz) + ((i // 2) % nz) * 2 + i // (2 * nz)
        limit = jnp.where((c >= 1) & (c < ctx), keep_count[c], 0)
        anchors = jnp.where(ctx >= 1, slots, 0)
        live = row_of < jnp.where(row_of < keep, limit, anchors)
        at = pl.ds(pl.multiple_of(i * slots, 16), slots)
        bias[at, :] = jnp.where(first_lane & jnp.logical_not(live), -1e30, 0.0).astype(BF)
        return carry

    lax.fori_loop(0, n_ctx, mark, 0)

    extra.second()
    parts[0].own()

    got_freq.wait()
    freq_row = freq_v[0:1, :]
    lane = lax.broadcasted_iota(jnp.int32, (1, HD), 1)
    sign = jnp.where(lane < HD // 2, -1.0, 1.0)

    def table_of(i, carry):
        at = pl.ds(pl.multiple_of(i * 64, 64), 64)
        places = (ctx * rows + i * 64 + lax.broadcasted_iota(jnp.int32, (64, HD), 0)).astype(F32)
        cos_t[at, :], sin_t[at, :] = tables(places, freq_row, sign)
        return carry

    lax.fori_loop(0, rows // 64, table_of, 0)
    extra_places = jnp.concatenate(
        [
            (ctx * rows + picked).astype(F32),
            (ctx * share + lax.broadcasted_iota(jnp.int32, (share, HD), 0)).astype(F32),
        ],
        axis=0,
    )
    extra_cos, extra_sin = tables(extra_places, freq_row, sign)

    extra.third()
    anchor_copy(0).wait_recv()
    for step in kv_near:
        send(anchor_slot, anchor_slot, {"kv": kv_at(*step)}, a_sem.at[2], a_sem.at[3])
    parts[1].own((0, 1))
    parts[0].second()
    extra.finish()
    all_shares = H.at[0:7, pl.ds(0, share)]
    take(all_shares, a_sem.at[3])
    def block_at(at_z, at_y):
        return pl.ds(pl.multiple_of(((core * nz + at_z) * 2 + at_y) * slots, slots), slots)

    take(W, l_sem.at[2])
    kv_cols = slice(groups * HD, (groups + 2) * HD)
    raw = jnp.zeros((slots, 2 * HD), F32)
    for s in range(n_src):
        raw += jnp.dot(RH[s], W[s * depth : (s + 1) * depth, kv_cols], preferred_element_type=F32)
    own_block = block_at(z, yh)
    G[own_block, 0:HD] = rope(raw[:, :HD], extra_cos, extra_sin).astype(BF)
    G[own_block, HD:] = raw[:, HD:].astype(BF)

    def hop(part, step, send_sem, recv_sem):
        send(part, part, {"ctx": ctx_at(*step)}, c_send.at[send_sem], c_recv.at[recv_sem])

    def at_z(dz):
        return G.at[pl.ds(pl.multiple_of((core * nz + (z + dz) % nz) * 2 * slots, 2 * slots), 2 * slots)]

    def to_core(part):
        hop(part, (0, 0, 1), 2, 8)

    near_z = ((2, 1), (nz - 2, 2), (1, 3), (nz - 1, 4))
    block = G.at[own_block]
    hop(block, (1, 0, 0), 0, 0)
    for dz, sem in near_z:
        hop(block, (0, dz, 0), 1, sem)
    parts[1].own((2,))

    def project(r):
        part = pl.ds(pl.multiple_of(r * chunk, chunk), chunk)
        raw = jnp.zeros((chunk, (groups + 2) * HD), F32)
        for s in range(n_src):
            raw += jnp.dot(H[s, part], W[s * depth : (s + 1) * depth], preferred_element_type=F32)
        cosine, sine = cos_t[part, :], sin_t[part, :]
        for g in range(groups):
            at = pl.ds(pl.multiple_of(r * many + g * chunk, chunk), chunk)
            Q[at, :] = rope(raw[:, g * HD : (g + 1) * HD], cosine, sine).astype(BF)
        KL[part, :] = rope(raw[:, groups * HD : (groups + 1) * HD], cosine, sine).astype(BF)
        VL[part, :] = raw[:, (groups + 1) * HD :].astype(BF)

    take(block, c_recv.at[0])
    block = G.at[block_at(z, 1 - yh)]
    for dz, sem in near_z:
        hop(block, (0, dz, 0), 1, sem)
    to_core(at_z(0))
    parts[0].third()
    parts[2].own()
    parts[1].second()
    for i, (dz, sem) in enumerate(near_z):
        got = at_z(nz - dz)
        take(got, c_recv.at[sem])
        if i < 2:
            hop(got, (0, (1, nz - 1)[i], 0), 1, 5 + i)
            hop(G.at[block_at((z + nz - dz) % nz, i)], (0, dz, 0), 1, 7)
        to_core(got)
    parts[0].finish()
    project(0)
    parts[1].third()
    parts[3].own()
    for i, dz in enumerate((3, nz - 3)):
        got = at_z(nz - dz)
        take(got, c_recv.at[5 + i])
        to_core(got)
    got = at_z(nz // 2)
    take(got, c_recv.at[7])
    to_core(got)
    parts[2].second()
    parts[1].finish()
    project(1)
    half_far = n_far // 2
    take(G.at[0:half_far], c_recv.at[8])

    contract = (((1,), (1,)), ((), ()))
    in_chunk = lax.broadcasted_iota(jnp.int32, (many, rows), 0) % chunk
    key_place = lax.broadcasted_iota(jnp.int32, (many, rows), 1)
    adds_bias = (lax.broadcasted_iota(jnp.int32, (many, HD), 1) == 0).astype(F32).astype(BF)
    tile = 512
    tiles = range(0, n_far, tile)
    some = many // 2

    def attend(r):
        q = Q[pl.ds(pl.multiple_of(r * many, many), many), :]
        q_wide = jnp.concatenate([q, adds_bias], axis=1)
        s = lax.dot_general(q, KL[...], contract, preferred_element_type=F32)
        s = jnp.where(key_place <= in_chunk + r * chunk, s, -jnp.inf)
        S[:, n_far:] = s
        top = lane_fold(jnp.maximum, s[:, HD:], s[:, :HD])
        for at in tiles:
            keys = jnp.concatenate([G[at : at + tile, :HD], bias[at : at + tile]], axis=1)
            s = lax.dot_general(q_wide, keys, contract, preferred_element_type=F32)
            S[:, at : at + tile] = s
            top = lane_fold(jnp.maximum, s, top)
        top = jnp.max(top, axis=1, keepdims=True) * SCALE
        part = pl.ds(pl.multiple_of(r * chunk, chunk), chunk)
        for row in range(0, many, some):
            mine = slice(row, row + some)
            total = jnp.zeros((some, HD), F32)
            for at in range(0, n_far + rows, tile):
                e = jnp.exp2(S[mine, at : at + tile] * SCALE - top[mine])
                S[mine, at : at + tile] = e
                total = lane_fold(jnp.add, e, total)
            part_of = 1.0 / jnp.sum(total, axis=1, keepdims=True)
            result = jnp.zeros((some, HD), F32)
            for at in range(0, n_far + rows, tile):
                weights = (S[mine, at : at + tile] * part_of).astype(BF)
                values = G[at : at + tile, HD:] if at < n_far else VL[at - n_far : at - n_far + tile]
                result += jnp.dot(weights, values, preferred_element_type=F32)
            result = result.astype(BF)
            for g in range(some // chunk):
                head = row // chunk + g
                out_v[part, head * HD : (head + 1) * HD] = result[g * chunk : (g + 1) * chunk]
        fetch(out_v.at[part], out.at[part], 3)

    def step(r, carry):
        @pl.when(r == 1)
        def _():
            parts[2].third()
            parts[3].second()

        pl.when(r == 2)(parts[3].third)
        attend(r)

        @pl.when((r == 1) | (r == 2))
        def _():
            take(H.at[0, pl.ds(0, chunk + 2 * parts[3].cut)], k_recv.at[r + 1, 6])
            project(r + 1)

        return carry

    lax.fori_loop(0, n_chunks, step, 0)

    take(out_v, l_sem.at[3])
    for part in [extra, *parts]:
        part.sent()
    take(all_shares, a_sem.at[2])
    take(G.at[0:slots], c_send.at[0])
    take(G.at[0 : 14 * slots], c_send.at[1])
    take(G.at[0:half_far], c_send.at[2])

    @pl.when(ctx == 0)
    def _():
        take(H.at[0, pl.ds(0, (n_ctx - 1) * share)], a_sem.at[0])


def per_device(n_kv, n_ctx, hidden, w_query, w_key, w_value, keep_rows, keep_count):
    rows, depth = hidden.shape
    keep = keep_rows.shape[0]
    groups = w_query.shape[1] // HD
    nz = n_ctx // 4
    share = rows // n_ctx
    slots = keep + share
    freq = 500000.0 ** (-(np.arange(HD // 2, dtype=np.float64) * 2.0 / HD))
    freq = jnp.asarray(np.broadcast_to(np.concatenate([freq, freq]), (8, HD)), F32)
    any_spec = pl.BlockSpec(memory_space=pl.ANY)
    smem = pl.BlockSpec(memory_space=pltpu.SMEM)
    n_far = n_ctx * slots
    return pl.pallas_call(
        functools.partial(kernel, (rows, keep, share, groups, n_ctx, nz)),
        out_shape=jax.ShapeDtypeStruct((rows, groups * HD), BF),
        in_specs=[any_spec] * 4 + [smem, smem, any_spec],
        out_specs=any_spec,
        scratch_shapes=[
            pltpu.VMEM((n_kv, rows, depth), BF),
            pltpu.VMEM((n_kv, slots, depth), BF),
            pltpu.VMEM((n_kv * depth, (groups + 2) * HD), BF),
            pltpu.VMEM((n_far, 2 * HD), BF),
            pltpu.VMEM((n_far, HD), BF),
            pltpu.VMEM((rows, HD), BF),
            pltpu.VMEM((rows, HD), BF),
            pltpu.VMEM((rows * groups, HD), BF),
            pltpu.VMEM((groups * 128, n_far + rows), F32),
            pltpu.VMEM((rows, HD), F32),
            pltpu.VMEM((rows, HD), F32),
            pltpu.VMEM((8, HD), F32),
            pltpu.VMEM((rows, groups * HD), BF),
            pltpu.SemaphoreType.DMA((rows // 128 + 1,)),
            pltpu.SemaphoreType.DMA((rows // 128 + 1, 7)),
            pltpu.SemaphoreType.DMA((4,)),
            pltpu.SemaphoreType.DMA((3,)),
            pltpu.SemaphoreType.DMA((9,)),
            pltpu.SemaphoreType.DMA((4,)),
        ],
        compiler_params=pltpu.CompilerParams(
            collective_id=0, has_side_effects=True, vmem_limit_bytes=58 << 20
        ),
        name="prefill",
    )(hidden, w_query, w_key, w_value, keep_rows, keep_count, freq)


def solution(mesh):
    in_specs = (P("ctx", "kv"), P(None, "kv"), P(None, "kv"), P(None, "kv"), P("ctx"), P())
    out_specs = P("ctx", "kv")
    step = functools.partial(per_device, mesh.shape["kv"], mesh.shape["ctx"])
    return jax.shard_map(step, mesh=mesh, in_specs=in_specs, out_specs=out_specs, check_vma=False)
```

time: 469 us -> 61.5 us (0.13)
  the two profiles are of different devices: /device:TPU:1 before, /device:TPU:16 now
where the time goes in v2:
time: 61.5 us; the launch traced here: 61.4 us
  Pallas kernels  59.5 us (97%)
  local copies, waits for them, and re-layouts  1.87 us (3%)
    pallas_call x1, Pallas kernels, per_device(): pl.pallas_call(functools.partial(kernel, (rows, keep, share, groups, n_ct...  59.5 us
    unnamed x1, local copies, waits for them, and re-layouts  1.87 us

profile of v2, /device:TPU:16, one launch (start us, length us, event | category | flops | bytes accessed | tf_op | source)
XLA Modules:
  0.0 61.4 jit_solution(1267435059631832572)
XLA Ops:
  0.0 59.5 %prefill.1 = bf16[512,512]{1,0:T(8,128)(2,1)} custom-call(bf16[512,512]{1,0:T(8,128)(2,1)} %hidden.1, bf16[4096,512]{1,0:T(8,128)(2,1)} %w_query.1, bf16[4096,128]{1,0:T(8,128)(2,1)} %w_key.1, bf16[4096,128]{1,0:T(8,128)(2,1)} %w_value.1, s32[64]{0:T(128)} %keep_rows.1, s32[32]{0:T(128)} %keep_count.1, f32[8,128]{1,0:T(8,128)} %constant.2.clone.freq), custom_call_target="tpu_custom_call" | custom-call | tf_op jit(solution)/shard_map/prefill/pallas_call | solution.py:400
  59.5 1.9 %copy.9 = bf16[512,512]{1,0:T(8,128)(2,1)} copy(bf16[512,512]{1,0:T(8,128)(2,1)} %prefill.1) | data formatting | bytes 1048576

commit v3 on v2

--- a/solution.py
+++ b/solution.py
@@ -34,6 +34,7 @@
 
 class Gather:
     def __init__(self, sems, index, like, buf, base, rows, cut, kv_at, source):
+        self.flip = index % 2
         self.buf, self.base, self.rows, self.cut, self.at, self.source = buf, base, rows, cut, kv_at, source
         self.send_sem, self.recv = sems[0].at[index], [sems[1].at[index, i] for i in range(7)]
         self.like = like
@@ -69,6 +70,8 @@
     def third(self):
         n, cut = self.rows, self.cut
         mid = cut + up16((n - cut) // 2)
+        if self.flip:
+            mid = n + cut - mid
         self.took(n - cut, 3)
         self.fwd(self.part(3, 1, cut, mid), 1, 0, 6)
         self.took(n - cut, 4)
@@ -157,7 +160,17 @@
         [(lanes + k * HD == picked).astype(F32).astype(BF) for k in range(rows // HD)], axis=1
     )
     own_here.wait()
-    RH[kv, 0:keep] = jnp.dot(one_hot, H[kv], preferred_element_type=F32).astype(BF)
+
+    has_extra = ctx != 0
+
+    @pl.when(has_extra)
+    def _():
+        RH[kv, 0:keep] = jnp.dot(one_hot, H[kv], preferred_element_type=F32).astype(BF)
+
+    @pl.when(ctx == 0)
+    def _():
+        RH[:, 0:keep] = jnp.zeros((n_src, keep, depth), BF)
+
 
     near = len(kv_near) + len(ctx_near)
     pl.semaphore_wait(barrier, jnp.where(ctx == 0, near + n_ctx - 1, near))
@@ -187,10 +200,10 @@
     sems = (k_send, k_recv)
     extra = Gather(sems, n_chunks, H, RH, 0, keep, keep // 2, kv_at, RH.at[kv, pl.ds(0, keep)])
     parts = [
-        Gather(sems, r, H, H, r * chunk, chunk, (48, 64)[r >= n_chunks // 2], kv_at, hidden.at[pl.ds(r * chunk, chunk)])
+        Gather(sems, r, H, H, r * chunk, chunk, (48 if r else 64), kv_at, hidden.at[pl.ds(r * chunk, chunk)])
         for r in range(n_chunks)
     ]
-    extra.own()
+    pl.when(has_extra)(extra.own)
 
     KL[...] = jnp.zeros_like(KL)
     VL[...] = jnp.zeros_like(VL)
@@ -208,7 +221,7 @@
 
     lax.fori_loop(0, n_ctx, mark, 0)
 
-    extra.second()
+    pl.when(has_extra)(extra.second)
     parts[0].own()
 
     got_freq.wait()
@@ -232,13 +245,13 @@
     )
     extra_cos, extra_sin = tables(extra_places, freq_row, sign)
 
-    extra.third()
+    pl.when(has_extra)(extra.third)
     anchor_copy(0).wait_recv()
     for step in kv_near:
         send(anchor_slot, anchor_slot, {"kv": kv_at(*step)}, a_sem.at[2], a_sem.at[3])
     parts[1].own((0, 1))
     parts[0].second()
-    extra.finish()
+    pl.when(has_extra)(extra.finish)
     all_shares = H.at[0:7, pl.ds(0, share)]
     take(all_shares, a_sem.at[3])
     def block_at(at_z, at_y):
@@ -262,10 +275,10 @@
     def to_core(part):
         hop(part, (0, 0, 1), 2, 8)
 
-    near_z = ((2, 1), (nz - 2, 2), (1, 3), (nz - 1, 4))
+    near_z = ((2, 1, 9), (nz - 2, 2, 10), (1, 3, 3), (nz - 1, 4, 4))
     block = G.at[own_block]
     hop(block, (1, 0, 0), 0, 0)
-    for dz, sem in near_z:
+    for dz, sem, _ in near_z:
         hop(block, (0, dz, 0), 1, sem)
     parts[1].own((2,))
 
@@ -283,22 +296,29 @@
 
     take(block, c_recv.at[0])
     block = G.at[block_at(z, 1 - yh)]
-    for dz, sem in near_z:
+    for dz, _, sem in near_z:
         hop(block, (0, dz, 0), 1, sem)
     to_core(at_z(0))
+
+    def onward(which):
+        at_y = (yh, 1 - yh)[which]
+        for i, (dz, *sems_z) in enumerate(near_z[:2]):
+            got = G.at[block_at((z + nz - dz) % nz, at_y)]
+            take(got, c_recv.at[sems_z[which]])
+            hop(got, (0, (1, nz - 1)[i], 0), 1, 5 + i)
+            if i == which:
+                hop(got, (0, dz, 0), 1, 7)
+
+    onward(0)
     parts[0].third()
     parts[2].own()
     parts[1].second()
-    for i, (dz, sem) in enumerate(near_z):
+    onward(1)
+    for dz, _, sem in near_z:
         got = at_z(nz - dz)
-        take(got, c_recv.at[sem])
-        if i < 2:
-            hop(got, (0, (1, nz - 1)[i], 0), 1, 5 + i)
-            hop(G.at[block_at((z + nz - dz) % nz, i)], (0, dz, 0), 1, 7)
+        if dz in (1, nz - 1):
+            take(got, c_recv.at[sem])
         to_core(got)
-    parts[0].finish()
-    project(0)
-    parts[1].third()
     parts[3].own()
     for i, dz in enumerate((3, nz - 3)):
         got = at_z(nz - dz)
@@ -307,9 +327,10 @@
     got = at_z(nz // 2)
     take(got, c_recv.at[7])
     to_core(got)
+    parts[1].third()
+    parts[0].finish()
+    project(0)
     parts[2].second()
-    parts[1].finish()
-    project(1)
     half_far = n_far // 2
     take(G.at[0:half_far], c_recv.at[8])
 
@@ -355,15 +376,16 @@
         fetch(out_v.at[part], out.at[part], 3)
 
     def step(r, carry):
-        @pl.when(r == 1)
+        attend(r)
+
+        @pl.when(r == 0)
         def _():
             parts[2].third()
             parts[3].second()
 
-        pl.when(r == 2)(parts[3].third)
-        attend(r)
-
-        @pl.when((r == 1) | (r == 2))
+        pl.when(r == 1)(parts[3].third)
+
+        @pl.when(r < n_chunks - 1)
         def _():
             take(H.at[0, pl.ds(0, chunk + 2 * parts[3].cut)], k_recv.at[r + 1, 6])
             project(r + 1)
@@ -373,7 +395,8 @@
     lax.fori_loop(0, n_chunks, step, 0)
 
     take(out_v, l_sem.at[3])
-    for part in [extra, *parts]:
+    pl.when(has_extra)(extra.sent)
+    for part in parts:
         part.sent()
     take(all_shares, a_sem.at[2])
     take(G.at[0:slots], c_send.at[0])
@@ -420,7 +443,7 @@
             pltpu.SemaphoreType.DMA((rows // 128 + 1, 7)),
             pltpu.SemaphoreType.DMA((4,)),
             pltpu.SemaphoreType.DMA((3,)),
-            pltpu.SemaphoreType.DMA((9,)),
+            pltpu.SemaphoreType.DMA((11,)),
             pltpu.SemaphoreType.DMA((4,)),
         ],
         compiler_params=pltpu.CompilerParams(

time: 61.5 us -> 59.5 us (0.967)
  the two profiles are of different devices: /device:TPU:16 before, /device:TPU:1 now
where the time goes in v3:
time: 59.5 us; the launch traced here: 58.6 us
  Pallas kernels  56.8 us (95%)
  local copies, waits for them, and re-layouts  1.87 us (3%)
    pallas_call x1, Pallas kernels, per_device(): pl.pallas_call(functools.partial(kernel, (rows, keep, share, groups, n_ct...  56.8 us
    unnamed x1, local copies, waits for them, and re-layouts  1.87 us

profile of v3, /device:TPU:1, one launch (start us, length us, event | category | flops | bytes accessed | tf_op | source)
XLA Modules:
  0.0 58.6 jit_solution(9393696665527109938)
XLA Ops:
  0.0 56.8 %prefill.1 = bf16[512,512]{1,0:T(8,128)(2,1)} custom-call(bf16[512,512]{1,0:T(8,128)(2,1)} %hidden.1, bf16[4096,512]{1,0:T(8,128)(2,1)} %w_query.1, bf16[4096,128]{1,0:T(8,128)(2,1)} %w_key.1, bf16[4096,128]{1,0:T(8,128)(2,1)} %w_value.1, s32[64]{0:T(128)} %keep_rows.1, s32[32]{0:T(128)} %keep_count.1, f32[8,128]{1,0:T(8,128)} %constant.2.clone.freq), custom_call_target="tpu_custom_call" | custom-call | tf_op jit(solution)/shard_map/prefill/pallas_call | solution.py:423
  56.8 1.9 %copy.9 = bf16[512,512]{1,0:T(8,128)(2,1)} copy(bf16[512,512]{1,0:T(8,128)(2,1)} %prefill.1) | data formatting | bytes 1048576

commit v4 on v3

--- a/solution.py
+++ b/solution.py
@@ -313,13 +313,15 @@
     parts[0].third()
     parts[2].own()
     parts[1].second()
+    parts[3].own()
     onward(1)
     for dz, _, sem in near_z:
         got = at_z(nz - dz)
         if dz in (1, nz - 1):
             take(got, c_recv.at[sem])
         to_core(got)
-    parts[3].own()
+    parts[0].finish()
+    project(0)
     for i, dz in enumerate((3, nz - 3)):
         got = at_z(nz - dz)
         take(got, c_recv.at[5 + i])
@@ -328,9 +330,8 @@
     take(got, c_recv.at[7])
     to_core(got)
     parts[1].third()
-    parts[0].finish()
-    project(0)
     parts[2].second()
+    parts[3].second()
     half_far = n_far // 2
     take(G.at[0:half_far], c_recv.at[8])
 
@@ -378,11 +379,7 @@
     def step(r, carry):
         attend(r)
 
-        @pl.when(r == 0)
-        def _():
-            parts[2].third()
-            parts[3].second()
-
+        pl.when(r == 0)(parts[2].third)
         pl.when(r == 1)(parts[3].third)
 
         @pl.when(r < n_chunks - 1)

time: 59.5 us -> 58.6 us (0.985); the launches traced: 58.6 us -> 58.5 us
  no operation moved by 1% of the time
where the time goes in v4:
time: 58.6 us; the launch traced here: 58.5 us
  Pallas kernels  56.6 us (97%)
  local copies, waits for them, and re-layouts  1.87 us (3%)
    pallas_call x1, Pallas kernels, per_device(): pl.pallas_call(functools.partial(kernel, (rows, keep, share, groups, n_ct...  56.6 us
    unnamed x1, local copies, waits for them, and re-layouts  1.87 us

profile of v4, /device:TPU:1, one launch (start us, length us, event | category | flops | bytes accessed | tf_op | source)
XLA Modules:
  0.0 58.5 jit_solution(552006103755636012)
XLA Ops:
  0.0 56.6 %prefill.1 = bf16[512,512]{1,0:T(8,128)(2,1)} custom-call(bf16[512,512]{1,0:T(8,128)(2,1)} %hidden.1, bf16[4096,512]{1,0:T(8,128)(2,1)} %w_query.1, bf16[4096,128]{1,0:T(8,128)(2,1)} %w_key.1, bf16[4096,128]{1,0:T(8,128)(2,1)} %w_value.1, s32[64]{0:T(128)} %keep_rows.1, s32[32]{0:T(128)} %keep_count.1, f32[8,128]{1,0:T(8,128)} %constant.2.clone.freq), custom_call_target="tpu_custom_call" | custom-call | tf_op jit(solution)/shard_map/prefill/pallas_call | solution.py:420
  56.6 1.9 %copy.9 = bf16[512,512]{1,0:T(8,128)(2,1)} copy(bf16[512,512]{1,0:T(8,128)(2,1)} %prefill.1) | data formatting | bytes 1048576

commit v5 on v4

--- a/solution.py
+++ b/solution.py
@@ -294,6 +294,7 @@
         KL[part, :] = rope(raw[:, groups * HD : (groups + 1) * HD], cosine, sine).astype(BF)
         VL[part, :] = raw[:, (groups + 1) * HD :].astype(BF)
 
+    parts[0].third()
     take(block, c_recv.at[0])
     block = G.at[block_at(z, 1 - yh)]
     for dz, _, sem in near_z:
@@ -310,7 +311,6 @@
                 hop(got, (0, dz, 0), 1, 7)
 
     onward(0)
-    parts[0].third()
     parts[2].own()
     parts[1].second()
     parts[3].own()

time: 58.6 us -> 58.6 us (level)
  no operation moved by 1% of the time
where the time goes in v5:
time: 58.6 us; the launch traced here: 58.5 us
  Pallas kernels  56.6 us (97%)
  local copies, waits for them, and re-layouts  1.87 us (3%)
    pallas_call x1, Pallas kernels, per_device(): pl.pallas_call(functools.partial(kernel, (rows, keep, share, groups, n_ct...  56.6 us
    unnamed x1, local copies, waits for them, and re-layouts  1.87 us

profile of v5, /device:TPU:1, one launch (start us, length us, event | category | flops | bytes accessed | tf_op | source)
XLA Modules:
  0.0 58.5 jit_solution(1020590884868589741)
XLA Ops:
  0.0 56.6 %prefill.1 = bf16[512,512]{1,0:T(8,128)(2,1)} custom-call(bf16[512,512]{1,0:T(8,128)(2,1)} %hidden.1, bf16[4096,512]{1,0:T(8,128)(2,1)} %w_query.1, bf16[4096,128]{1,0:T(8,128)(2,1)} %w_key.1, bf16[4096,128]{1,0:T(8,128)(2,1)} %w_value.1, s32[64]{0:T(128)} %keep_rows.1, s32[32]{0:T(128)} %keep_count.1, f32[8,128]{1,0:T(8,128)} %constant.2.clone.freq), custom_call_target="tpu_custom_call" | custom-call | tf_op jit(solution)/shard_map/prefill/pallas_call | solution.py:420
  56.6 1.9 %copy.9 = bf16[512,512]{1,0:T(8,128)(2,1)} copy(bf16[512,512]{1,0:T(8,128)(2,1)} %prefill.1) | data formatting | bytes 1048576
